TPU v7x, 32 devices: a whole 2x2x4 slice. The times are simulated.
32 devices in a mesh: epoch: 8 (over z, y), col: 4 (over x, core).
Axes of the slice: x: 2, y: 2, z: 4, core: 2. Of those that a mesh axis runs over, the one named last changes fastest.
Arguments:
- partials: bfloat16 [2048, 8192], P('epoch', 'col'), may hold values from -6 to 6
- gaps: int32 [2048], P('epoch'), may hold values 0 or 1
- arc_start: int32 [1], replicated, may hold values from 512 to 1535
- taps: bfloat16 [241], replicated, may hold values from -0.375 to 0.375
Outputs:
- normal_matrix: float32 [8192, 8192], P('col', 'epoch')
All inputs are finite; a program needn't handle non-finite values. No bound on the sum of `gaps` on one device may be relied on, other than what follows from the above.
Results may differ from a plain program's by a relative error of at most 0.0026.
Values may be sent and summed in bfloat16 or wider, within the bound.
A program may use at most 64 MiB of HBM per device.

v0:
```python
import jax
import jax.numpy as jnp
from jax import lax
from jax.sharding import PartitionSpec as P


def shifted(block, axis, distance):
    devices = range(lax.axis_size(axis))
    route = [(i - distance, i) for i in devices if i - distance in devices]
    return lax.ppermute(block, axis, route)


def filter_table(first, rows, halo, taps, boundary):
    width = rows + halo
    padded_taps = jnp.concatenate([taps[::-1], jnp.zeros((rows,), taps.dtype)], axis=0)
    values = jnp.tile(padded_taps, rows)[: rows * width].reshape(rows, width)
    later = jnp.arange(rows, dtype=jnp.int32)
    source = jnp.arange(width, dtype=jnp.int32)
    lag = later[:, None] + halo - source[None, :]
    arc_later = first + later >= boundary
    arc_source = first - halo + source >= boundary
    keep = (lag >= 0) & (lag <= halo) & (arc_later[:, None] == arc_source[None, :])
    return jnp.where(keep, values, jnp.zeros_like(values))


def on_device(partials, gaps, arc_start, taps):
    rows = partials.shape[0]
    halo = taps.shape[0] - 1
    masked = partials * gaps[:, None].astype(jnp.bfloat16)
    earlier = shifted(masked[rows - halo :], "epoch", 1)
    first = lax.axis_index("epoch") * rows
    table = filter_table(first, rows, halo, taps, arc_start[0])
    inner = jnp.dot(table[:, halo:], masked, preferred_element_type=jnp.float32)
    edge = jnp.dot(table[:, :halo], earlier, preferred_element_type=jnp.float32)
    white = (inner + edge).astype(jnp.bfloat16)
    scale_factor = (rows * lax.axis_size("epoch")) ** (-0.5)
    contract = (((0,), (0,)), ((), ()))
    widened = lax.all_gather(white, "col", axis=1, tiled=True)
    right_cols = lax.all_to_all(widened, "epoch", split_axis=1, concat_axis=0, tiled=True)
    left_cols = lax.all_gather(white, "epoch", axis=0, tiled=True)
    gram = lax.dot_general(left_cols, right_cols, contract, preferred_element_type=jnp.float32)
    return gram * scale_factor


def solution(mesh):
    in_specs = (P("epoch", "col"), P("epoch"), P(), P())
    out_specs = P("col", "epoch")
    return jax.shard_map(
        on_device, mesh=mesh, in_specs=in_specs, out_specs=out_specs, check_vma=False
    )
```

profile of v0, /device:TPU:24, one launch (start us, length us, event | category | flops | bytes accessed | tf_op | source)
XLA Modules:
  0.0 294.7 jit_solution(16377663338441644546)
XLA Ops:
  6.5 0.0 all-gather.5.cloned.1.call-start
  6.5 0.7 convert_element_type.7
  7.2 1.4 broadcast_multiply_fusion
  8.6 1.0 slice.19
  9.6 3.4 %collective-permute-start = (bf16[240,2048]{1,0:T(8,128)(2,1)}, bf16[240,2048]{1,0:T(8,128)(2,1)S(1)}, u32[]{:S(2)}, u32[]{:S(2)}) collective-permute-start(bf16[240,2048]{1,0:T(8,128)(2,1)} %slice.19), channel_id=1, source_target_pairs={{0,4},{4,8},{8,12},{12,16},{16,20},{20,24},{24,28},{1,5},{5,9},{9,... | collective-permute-start | bytes 2949128 | tf_op jit(solution)/shard_map/ppermute | solution.py:10
  13.7 0.7 reverse
  14.4 0.1 slice.24
  14.5 0.5 tile.10
  15.0 0.5 reshape.24
  15.6 0.2 fusion.5
  15.9 0.5 fusion.7
  16.3 19.7 %collective-permute-done = bf16[240,2048]{1,0:T(8,128)(2,1)S(1)} collective-permute-done((bf16[240,2048]{1,0:T(8,128)(2,1)}, bf16[240,2048]{1,0:T(8,128)(2,1)S(1)}, u32[]{:S(2)}, u32[]{:S(2)}) %collective-permute-start) | collective-permute-done | bytes 983072 | tf_op jit(solution)/shard_map/ppermute | solution.py:10
  36.1 1.4 fusion
  37.5 0.0 all-gather.5.cloned.1.call-update
  37.5 0.0 all-gather.3.cloned.1.call-start
  37.6 0.7 all-gather.3.cloned.1.call-update
  38.3 34.0 %all-gather.5.cloned.1.call-done = bf16[256,8192]{1,0:T(8,128)(2,1)} async-done(((bf16[256,2048]{1,0:T(8,128)(2,1)}), bf16[256,8192]{1,0:T(8,128)(2,1)}) %all-gather.5.cloned.1.call-update) | async-done | bytes 4194320 | tf_op jit(solution)/shard_map/all_gather | solution.py:38
  72.2 2.6 copy.8
  74.9 188.6 %all_to_all.19 = bf16[256,8,1024]{2,0,1:T(8,128)(2,1)} all-to-all(bf16[256,8,1024]{2,0,1:T(8,128)(2,1)S(1)} %bitcast.15), channel_id=1, replica_groups=mesh['epoch'=8,'col'=4] {'epoch'}, dimensions={1} | all-to-all | bytes 8388608 | tf_op jit(solution)/shard_map/all_to_all | solution.py:39
  263.5 9.7 %all-gather.3.cloned.1.call-done = bf16[2048,2048]{1,0:T(8,128)(2,1)} async-done(((bf16[256,2048]{1,0:T(8,128)(2,1)}), bf16[2048,2048]{1,0:T(8,128)(2,1)}) %all-gather.3.cloned.1.call-update) | async-done | bytes 8388624 | tf_op jit(solution)/shard_map/all_gather | solution.py:40
  273.2 14.6 %convolution_multiply_fusion = f32[2048,1024]{1,0:T(8,128)} fusion(bf16[2048,2048]{1,0:T(8,128)(2,1)} %all-gather.3.cloned.1.call-done, bf16[2048,1024]{1,0:T(8,128)(2,1)} %bitcast.17), kind=kOutput, calls=%fused_computation | convolution fusion | flops 8592031744 | bytes 20971520 | tf_op jit(solution)/shard_map/dot_general | solution.py:41
  (6 shorter events, 0.1 us)
Async XLA Ops:
  6.5 65.7 %all-gather.5.cloned.1.call-start = ((), (), s32[]{:S(2)}) async-start(), calls=%async_computation.2 | async-start | bytes 5242880 | tf_op jit(solution)/shard_map/all_gather | solution.py:38
  9.6 26.5 %collective-permute-start = (bf16[240,2048]{1,0:T(8,128)(2,1)}, bf16[240,2048]{1,0:T(8,128)(2,1)S(1)}, u32[]{:S(2)}, u32[]{:S(2)}) collective-permute-start(bf16[240,2048]{1,0:T(8,128)(2,1)} %slice.19), channel_id=1, source_target_pairs={{0,4},{4,8},{8,12},{12,16},{16,20},{20,24},{24,28},{1,5},{5,9},{9,... | collective-permute-start | bytes 2949128 | tf_op jit(solution)/shard_map/ppermute | solution.py:10
  37.5 235.7 %all-gather.3.cloned.1.call-start = ((), (), s32[]{:S(2)}) async-start(), calls=%async_computation.1 | async-start | bytes 9437184 | tf_op jit(solution)/shard_map/all_gather | solution.py:40
Sparse Core Ops, SparseCore 0:
  37.7 34.5 all-gather.4
  74.4 198.7 all-gather.2
where the time goes:
time: 299 us; the launch traced here: 295 us
  blocking collectives  189 us (63%)
  waiting for transfers between devices  64.2 us (21%)
  matrix products  16.5 us (6%)
  between operations  14.1 us (5%)
  local copies, waits for them, and re-layouts  5.51 us (2%)
  starting transfers between devices  3.46 us (1%)
    all_to_all x1, blocking collectives, on_device(): lax.all_to_all(widened, 'epoch', split_axis=1, concat_axis=0, tiled=True)  189 us
    all_gather x1, waiting for transfers between devices, on_device(): widened = lax.all_gather(white, 'col', axis=1, tiled=True)  34 us
    ppermute x1, waiting for transfers between devices, shifted(): return lax.ppermute(block, axis, route)  19.7 us
    dot_general x1, matrix products, on_device(): lax.dot_general(left_cols, right_cols, contract, preferred_element_type=j...  14.6 us
    all_gather x1, waiting for transfers between devices, on_device(): left_cols = lax.all_gather(white, 'epoch', axis=0, tiled=True)  9.74 us
  transfers between devices with their start and end apart: 3, of which 3 were waited for; matrix products, arithmetic and copies ran while one was open for 2% of the time, Pallas kernels for 0%

commit v1 on v0

v1 whole, which is shorter than its diff:
```python
import functools

import jax
import jax.numpy as jnp
from jax import lax
from jax.experimental import pallas as pl
from jax.experimental.pallas import tpu as pltpu
from jax.sharding import PartitionSpec as P

MESH = pl.DeviceIdType.MESH
CHUNKS = 4


def kernel(
    ne, nc, arc_ref, gaps_ref, taps_ref, part_ref, out_ref,
    left, right, table, wl, wr,
    left_recv, right_recv, up_send, dn_send, y_send, sib_send, x_send,
):
    rows, width = part_ref.shape
    rwidth = right.shape[2]
    nz, nh = ne // 2, nc // 2
    G = CHUNKS
    crows = rows // G
    e, c = lax.axis_index("epoch"), lax.axis_index("col")
    z, y = e // 2, e % 2
    h, k = c // 2, c % 2
    src = e * nc // ne
    h_src, k_src = src // 2, src % 2
    offset = pl.multiple_of((e * nc % ne) // nc * rwidth, rwidth)
    is_src = c == src
    is_relay = jnp.logical_and(k == k_src, h != h_src)
    has_up, has_dn = z < nz - 1, z > 0
    up, dn, across, sib = e + 2, e - 2, e + 1 - 2 * y, c + 1 - 2 * k

    barrier = pltpu.get_barrier_semaphore()

    def greet(ee, cc):
        pl.semaphore_signal(barrier, inc=1, device_id=(ee, cc), device_id_type=MESH)

    @pl.when(has_up)
    def _():
        greet(up, c)

    @pl.when(has_dn)
    def _():
        greet(dn, c)

    greet(across, c)
    greet(e, sib)
    for i in range(1, nh):
        greet(e, lax.rem(h + i, nh) * 2 + k)

    eye = lax.broadcasted_iota(jnp.int32, (rows, rows), 0) == lax.broadcasted_iota(jnp.int32, (rows, rows), 1)
    column = jnp.sum(jnp.where(eye, gaps_ref[...].astype(jnp.float32), 0.0), axis=1, keepdims=True)
    left[e] = part_ref[...] * column.astype(jnp.bfloat16)

    pl.semaphore_wait(barrier, 1 + nh + has_up.astype(jnp.int32) + has_dn.astype(jnp.int32))

    def piece(buf, b, g):
        return buf.at[b, pl.ds(pl.multiple_of(g * crows, crows), crows)]

    def send_left(b, g, sem, ee):
        pltpu.make_async_remote_copy(
            src_ref=piece(left, b, g), dst_ref=piece(left, b, g),
            send_sem=sem.at[b], recv_sem=left_recv.at[b, g],
            device_id=(ee, c), device_id_type=MESH,
        ).start()

    def right_source(b, g):
        return left.at[b, pl.ds(pl.multiple_of(g * crows, crows), crows), pl.ds(offset, rwidth)]

    def send_right(source, b, g, sem, cc):
        pltpu.make_async_remote_copy(
            src_ref=source, dst_ref=piece(right, b, g),
            send_sem=sem, recv_sem=right_recv.at[b, g],
            device_id=(e, cc), device_id_type=MESH,
        ).start()

    def spread(b, g):
        @pl.when(is_src)
        def _():
            pltpu.make_async_copy(right_source(b, g), piece(right, b, g), right_recv.at[b, g]).start()
            for i in range(1, nh):
                send_right(right_source(b, g), b, g, x_send.at[b, i - 1], lax.rem(h + i, nh) * 2 + k)
            send_right(right_source(b, g), b, g, sib_send.at[b], sib)

    def wait_left(b, g):
        pltpu.make_async_copy(piece(left, b, g), piece(left, b, g), left_recv.at[b, g]).wait()

    def wait_right(b, g):
        pltpu.make_async_copy(piece(right, b, g), piece(right, b, g), right_recv.at[b, g]).wait()

        @pl.when(is_relay)
        def _():
            send_right(piece(right, b, g), b, g, sib_send.at[b], sib)

    def slab(t):
        both = 2 * jnp.minimum(z, nz - 1 - z)
        alternate = jnp.where(t % 2 == 1, z - (t + 1) // 2, z + t // 2)
        rest = jnp.where(z <= nz - 1 - z, t, nz - 1 - t)
        return jnp.where(t <= both, alternate, rest)

    def own(g, carry):
        @pl.when(has_up)
        def _():
            send_left(e, g, up_send, up)

        @pl.when(has_dn)
        def _():
            send_left(e, g, dn_send, dn)

        send_left(e, g, y_send, across)
        spread(e, g)
        return carry

    lax.fori_loop(0, G, own, 0)

    table[...] = pltpu.roll(
        jnp.broadcast_to(taps_ref[...], (rows, 2 * rows)), 0, 1, stride=1, stride_axis=0
    )
    out_ref[...] = jnp.zeros_like(out_ref)

    def whiten_and_add(b):
        first = b * rows
        before = jnp.maximum(b - 1, 0)
        later = first + lax.broadcasted_iota(jnp.int32, (rows, 2 * rows), 0)
        source = first - rows + lax.broadcasted_iota(jnp.int32, (rows, 2 * rows), 1)
        boundary = arc_ref[0]
        same = (later >= boundary) == (source >= boundary)
        keep = jnp.logical_and(same, source >= 0)
        taps = jnp.where(keep, table[...], 0.0).astype(jnp.bfloat16)
        edge, inner = taps[:, :rows], taps[:, rows:]

        def whiten(buf, into, step):
            @pl.loop(0, into.shape[1] // step)
            def _(i):
                cols = pl.ds(pl.multiple_of(i * step, step), step)
                white = jnp.dot(inner, buf[b, :, cols], preferred_element_type=jnp.float32)
                white += jnp.dot(edge, buf[before, :, cols], preferred_element_type=jnp.float32)
                into[:, cols] = white.astype(jnp.bfloat16)

        whiten(left, wl, min(512, width))
        whiten(right, wr, min(512, rwidth))

        @pl.loop(0, width // 256)
        def _(i):
            cols = pl.ds(pl.multiple_of(i * 256, 256), 256)
            out_ref[cols, :] += lax.dot_general(
                wl[:, cols], wr[...], (((0,), (0,)), ((), ())), preferred_element_type=jnp.float32
            )

    def step(it, carry):
        t, g = it // G, it % G
        moving = t < nz

        @pl.when(jnp.logical_and(moving, z - t - 1 >= 0))
        def _():
            b = e - 2 * (t + 1)
            wait_left(b, g)

            @pl.when(has_up)
            def _():
                send_left(b, g, up_send, up)

            spread(b, g)

        @pl.when(jnp.logical_and(moving, z + t + 1 < nz))
        def _():
            b = e + 2 * (t + 1)
            wait_left(b, g)

            @pl.when(has_dn)
            def _():
                send_left(b, g, dn_send, dn)

            spread(b, g)

        @pl.when(t + 1 < nz)
        def _():
            send_left(2 * slab(t + 1) + y, g, y_send, across)

        @pl.when(moving)
        def _():
            b = 2 * slab(t) + 1 - y
            wait_left(b, g)
            spread(b, g)

        @pl.when(t == 0)
        def _():
            wait_right(e, g)

        last = jnp.maximum(it - 1, 0)
        pt, pg = last // G, last % G
        passed = jnp.logical_and(it >= 1, pt < nz)

        @pl.when(jnp.logical_and(passed, z - pt - 1 >= 0))
        def _():
            wait_right(e - 2 * (pt + 1), pg)

        @pl.when(jnp.logical_and(passed, z + pt + 1 < nz))
        def _():
            wait_right(e + 2 * (pt + 1), pg)

        @pl.when(passed)
        def _():
            wait_right(2 * slab(pt) + 1 - y, pg)

        s = slab(jnp.maximum(t - 1, 0))
        s_now = slab(jnp.minimum(t, nz - 1))
        below = s < z
        post_a = jnp.where(s > z, 2 * s + 1 - y, 2 * s + 1)
        post_b = jnp.where(
            s > z,
            2 * s + 1,
            jnp.where(jnp.logical_and(below, y == 0), 2 * s + 2, 0),
        )
        valid_b = jnp.where(
            s > z,
            y == 1,
            jnp.where(below, jnp.logical_or(y == 0, s == 0), s == 0),
        )
        pre = jnp.where(s_now > z, 2 * s_now, jnp.where(y == 0, 0, 2 * s_now + 2))
        valid_pre = jnp.where(
            s_now > z, y == 0, jnp.logical_and(s_now < z, jnp.logical_or(y == 1, s_now == 0))
        )
        task = jnp.where(g == 0, post_a, jnp.where(g == 1, post_b, pre))
        valid = jnp.logical_or(
            jnp.logical_and(t >= 1, jnp.logical_or(g == 0, jnp.logical_and(g == 1, valid_b))),
            jnp.logical_and(jnp.logical_and(moving, t >= 1), jnp.logical_and(g == 2, valid_pre)),
        )

        @pl.when(valid)
        def _():
            whiten_and_add(task)

        return carry

    lax.fori_loop(0, nz * G + 2, step, 0)

    def drain(b, carry):
        def sent(buf, sem):
            pltpu.make_async_copy(buf.at[b], buf.at[b], sem).wait()

        mine = b % 2 == y

        @pl.when(jnp.logical_and(mine, jnp.logical_and(has_up, b <= e)))
        def _():
            sent(left, up_send.at[b])

        @pl.when(jnp.logical_and(mine, jnp.logical_and(has_dn, b >= e)))
        def _():
            sent(left, dn_send.at[b])

        @pl.when(mine)
        def _():
            sent(left, y_send.at[b])

        @pl.when(is_src)
        def _():
            for i in range(1, nh):
                sent(right, x_send.at[b, i - 1])

        @pl.when(jnp.logical_or(is_src, is_relay))
        def _():
            sent(right, sib_send.at[b])

        return carry

    lax.fori_loop(0, ne, drain, 0)


def on_device(ne, nc, partials, gaps, arc_start, taps):
    rows, width = partials.shape
    rwidth = width * nc // ne
    halo = taps.shape[0] - 1
    lags = jnp.pad(taps[::-1].astype(jnp.float32), (rows - halo, rows - 1))[None, :]
    vmem = pl.BlockSpec(memory_space=pltpu.VMEM)
    gram = pl.pallas_call(
        functools.partial(kernel, ne, nc),
        out_shape=jax.ShapeDtypeStruct((width, rwidth), jnp.float32),
        in_specs=[pl.BlockSpec(memory_space=pltpu.SMEM), vmem, vmem, vmem],
        out_specs=vmem,
        scratch_shapes=[
            pltpu.VMEM((ne, rows, width), jnp.bfloat16),
            pltpu.VMEM((ne, rows, rwidth), jnp.bfloat16),
            pltpu.VMEM((rows, 2 * rows), jnp.float32),
            pltpu.VMEM((rows, width), jnp.bfloat16),
            pltpu.VMEM((rows, rwidth), jnp.bfloat16),
            pltpu.SemaphoreType.DMA((ne, CHUNKS)),
            pltpu.SemaphoreType.DMA((ne, CHUNKS)),
            pltpu.SemaphoreType.DMA((ne,)),
            pltpu.SemaphoreType.DMA((ne,)),
            pltpu.SemaphoreType.DMA((ne,)),
            pltpu.SemaphoreType.DMA((ne,)),
            pltpu.SemaphoreType.DMA((ne, nc // 2)),
        ],
        compiler_params=pltpu.CompilerParams(
            collective_id=0, has_side_effects=True, vmem_limit_bytes=48 * 1024 * 1024
        ),
        cost_estimate=pl.CostEstimate(
            flops=2 * ne * rows * width * rwidth, bytes_accessed=4 * width * rwidth, transcendentals=0
        ),
    )(arc_start, gaps[None, :], lags, partials)
    return gram * (rows * ne) ** (-0.5)


def solution(mesh):
    in_specs = (P("epoch", "col"), P("epoch"), P(), P())
    out_specs = P("col", "epoch")
    ne, nc = mesh.shape["epoch"], mesh.shape["col"]
    return jax.shard_map(
        functools.partial(on_device, ne, nc),
        mesh=mesh, in_specs=in_specs, out_specs=out_specs, check_vma=False,
    )
```

time: 299 us -> 126 us (0.42)
  the two profiles are of different devices: /device:TPU:24 before, /device:TPU:17 now
where the time goes in v1:
time: 126 us
  Pallas kernels  114 us (90%)
  other arithmetic  8.86 us (7%)
  local copies, waits for them, and re-layouts  2.73 us (2%)
    pallas_call x1, Pallas kernels, on_device(): pl.pallas_call(functools.partial(kernel, ne, nc), out_shape=jax.ShapeDtyp...  114 us
    mul x1, other arithmetic, on_device(): return gram * (rows * ne) ** (-0.5)  8.78 us
    unnamed x6, local copies, waits for them, and re-layouts  2.73 us

profile of v1, /device:TPU:17, one launch (start us, length us, event | category | flops | bytes accessed | tf_op | source)
XLA Modules:
  0.0 126.1 jit_solution(7878341536498696724)
XLA Ops:
  0.7 0.7 reverse
  1.4 0.1 slice
  1.5 0.1 pad_convert_fusion
  1.6 0.0 copy-start
  1.6 1.2 copy-done
  2.8 0.0 copy-start.1
  2.8 0.7 copy-done.1
  3.5 113.9 %shard_map.46 = f32[2048,1024]{1,0:T(8,128)} custom-call(s32[1]{0:T(128)S(6)} %copy.5.arc_ref, s32[1,256]{1,0:T(1,128)S(1)} %bitcast.4, f32[1,512]{1,0:T(1,128)S(1)} %bitcast.3, bf16[256,2048]{1,0:T(8,128)(2,1)S(1)} %copy-done), custom_call_target="tpu_custom_call" | custom-call | flops 8589934592 | bytes 8388608 | tf_op jit(solution)/shard_map/pallas_call | solution.py:278
  117.4 8.8 %broadcast_multiply_fusion = f32[2048,1024]{1,0:T(8,128)} fusion(f32[2048,1024]{1,0:T(8,128)} %shard_map.46), kind=kLoop, calls=%fused_computation | loop fusion | flops 2097152 | bytes 16777216 | tf_op jit(solution)/shard_map/mul | solution.py:304
Async XLA Ops:
  1.6 1.2 copy-start
  2.8 0.7 copy-start.1

commit v2 on v1

--- a/solution.py
+++ b/solution.py
@@ -13,8 +13,8 @@
 
 def kernel(
     ne, nc, arc_ref, gaps_ref, taps_ref, part_ref, out_ref,
-    left, right, table, wl, wr,
-    left_recv, right_recv, up_send, dn_send, y_send, sib_send, x_send,
+    left, right, table, wl, wr, gaps_here, taps_here,
+    left_recv, right_recv, up_send, dn_send, y_send, sib_send, x_send, in_sem,
 ):
     rows, width = part_ref.shape
     rwidth = right.shape[2]
@@ -32,6 +32,19 @@
     has_up, has_dn = z < nz - 1, z > 0
     up, dn, across, sib = e + 2, e - 2, e + 1 - 2 * y, c + 1 - 2 * k
 
+    low, high = z == 0, z == nz - 1
+    near_low, near_high = z == 1, z == nz - 2
+    end, near = jnp.logical_or(low, high), jnp.logical_or(near_low, near_high)
+    slabs = jnp.where(near, nz - 1, nz)
+    far = jnp.where(z <= 1, nz - 1, 0)
+    beside = jnp.where(z <= 1, 0, nz - 1)
+
+    load_rows = pltpu.make_async_copy(part_ref, left.at[e], in_sem.at[0])
+    load_gaps = pltpu.make_async_copy(gaps_ref, gaps_here, in_sem.at[1])
+    load_taps = pltpu.make_async_copy(taps_ref, taps_here, in_sem.at[2])
+    load_rows.start()
+    load_gaps.start()
+    load_taps.start()
     barrier = pltpu.get_barrier_semaphore()
 
     def greet(ee, cc):
@@ -50,9 +63,12 @@
     for i in range(1, nh):
         greet(e, lax.rem(h + i, nh) * 2 + k)
 
+    load_rows.wait()
+    load_gaps.wait()
+    load_taps.wait()
     eye = lax.broadcasted_iota(jnp.int32, (rows, rows), 0) == lax.broadcasted_iota(jnp.int32, (rows, rows), 1)
-    column = jnp.sum(jnp.where(eye, gaps_ref[...].astype(jnp.float32), 0.0), axis=1, keepdims=True)
-    left[e] = part_ref[...] * column.astype(jnp.bfloat16)
+    column = jnp.sum(jnp.where(eye, gaps_here[...].astype(jnp.float32), 0.0), axis=1, keepdims=True)
+    left[e] = left[e] * column.astype(jnp.bfloat16)
 
     pl.semaphore_wait(barrier, 1 + nh + has_up.astype(jnp.int32) + has_dn.astype(jnp.int32))
 
@@ -98,7 +114,8 @@
         both = 2 * jnp.minimum(z, nz - 1 - z)
         alternate = jnp.where(t % 2 == 1, z - (t + 1) // 2, z + t // 2)
         rest = jnp.where(z <= nz - 1 - z, t, nz - 1 - t)
-        return jnp.where(t <= both, alternate, rest)
+        middle = jnp.where(t <= both, alternate, rest)
+        return jnp.where(z <= 1, z + t, jnp.where(z >= nz - 2, z - t, middle))
 
     def own(g, carry):
         @pl.when(has_up)
@@ -115,9 +132,10 @@
 
     lax.fori_loop(0, G, own, 0)
 
-    table[...] = pltpu.roll(
-        jnp.broadcast_to(taps_ref[...], (rows, 2 * rows)), 0, 1, stride=1, stride_axis=0
+    lags = pltpu.roll(
+        jnp.broadcast_to(taps_here[...], (2 * rows, 2 * rows)), 0, 1, stride=1, stride_axis=0
     )
+    table[...] = lags[:, :rows].T
     out_ref[...] = jnp.zeros_like(out_ref)
 
     def whiten_and_add(b):
@@ -175,13 +193,32 @@
 
             spread(b, g)
 
-        @pl.when(t + 1 < nz)
+        by_y = jnp.logical_or(t + 1 < nz - 1, jnp.logical_or(jnp.logical_not(end), g < G // 2))
+
+        @pl.when(jnp.logical_and(t + 1 < slabs, by_y))
         def _():
             send_left(2 * slab(t + 1) + y, g, y_send, across)
 
-        @pl.when(moving)
+        @pl.when(t < slabs)
         def _():
             b = 2 * slab(t) + 1 - y
+            wait_left(b, g)
+            to_near = jnp.logical_and(end, t == 0)
+            to_end = jnp.logical_and(near, jnp.logical_and(t == nz - 2, g >= G // 2))
+
+            @pl.when(jnp.logical_or(jnp.logical_and(low, to_near), jnp.logical_and(near_high, to_end)))
+            def _():
+                send_left(b, g, up_send, up)
+
+            @pl.when(jnp.logical_or(jnp.logical_and(high, to_near), jnp.logical_and(near_low, to_end)))
+            def _():
+                send_left(b, g, dn_send, dn)
+
+            spread(b, g)
+
+        @pl.when(jnp.logical_and(near, t == 1))
+        def _():
+            b = 2 * beside + 1 - y
             wait_left(b, g)
             spread(b, g)
 
@@ -201,12 +238,16 @@
         def _():
             wait_right(e + 2 * (pt + 1), pg)
 
-        @pl.when(passed)
+        @pl.when(jnp.logical_and(it >= 1, pt < slabs))
         def _():
             wait_right(2 * slab(pt) + 1 - y, pg)
 
-        s = slab(jnp.maximum(t - 1, 0))
-        s_now = slab(jnp.minimum(t, nz - 1))
+        @pl.when(jnp.logical_and(it >= 1, jnp.logical_and(near, pt == 1)))
+        def _():
+            wait_right(2 * beside + 1 - y, pg)
+
+        s = slab(jnp.clip(t - 1, 0, slabs - 1))
+        s_now = slab(jnp.minimum(t, slabs - 1))
         below = s < z
         post_a = jnp.where(s > z, 2 * s + 1 - y, 2 * s + 1)
         post_b = jnp.where(
@@ -223,11 +264,34 @@
         valid_pre = jnp.where(
             s_now > z, y == 0, jnp.logical_and(s_now < z, jnp.logical_or(y == 1, s_now == 0))
         )
+        free = jnp.where(near_low == (y == 0), 1, 2)
+        early = jnp.logical_and(t == 1, g == 3)
+        middling = jnp.logical_and(t == 2, g == free)
+        late = jnp.logical_and(t == 2, g == 3)
+        first_low = jnp.where(y == 0, 0, 2)
+        middling_low, late_low = jnp.where(y == 0, 2, 0), 1
+        middling_high, late_high = ne - 2, ne - 1
+        extra = jnp.where(
+            near_low,
+            jnp.where(early, first_low, jnp.where(late, late_low, middling_low)),
+            jnp.where(jnp.logical_or(early, middling), middling_high, late_high),
+        )
+        valid_extra = jnp.where(
+            near_low,
+            jnp.logical_or(early, jnp.logical_or(middling, late)),
+            jnp.logical_and(
+                near_high,
+                jnp.logical_or(late, jnp.where(y == 0, early, middling)),
+            ),
+        )
+        valid_post = jnp.logical_and(
+            jnp.logical_and(t >= 1, t <= slabs),
+            jnp.logical_or(g == 0, jnp.logical_and(g == 1, valid_b)),
+        )
+        valid_pre = jnp.logical_and(jnp.logical_and(t >= 1, t < slabs), jnp.logical_and(g == 2, valid_pre))
         task = jnp.where(g == 0, post_a, jnp.where(g == 1, post_b, pre))
-        valid = jnp.logical_or(
-            jnp.logical_and(t >= 1, jnp.logical_or(g == 0, jnp.logical_and(g == 1, valid_b))),
-            jnp.logical_and(jnp.logical_and(moving, t >= 1), jnp.logical_and(g == 2, valid_pre)),
-        )
+        task = jnp.where(valid_extra, extra, task)
+        valid = jnp.logical_or(valid_extra, jnp.logical_or(valid_post, valid_pre))
 
         @pl.when(valid)
         def _():
@@ -238,22 +302,40 @@
     lax.fori_loop(0, nz * G + 2, step, 0)
 
     def drain(b, carry):
-        def sent(buf, sem):
-            pltpu.make_async_copy(buf.at[b], buf.at[b], sem).wait()
+        def sent(buf, sem, part=rows):
+            span = buf.at[b, pl.ds(0, part)]
+            pltpu.make_async_copy(span, span, sem).wait()
 
         mine = b % 2 == y
-
-        @pl.when(jnp.logical_and(mine, jnp.logical_and(has_up, b <= e)))
+        whole_b = jnp.logical_and(end, b == e + 1 - 2 * y)
+        half_b = jnp.logical_and(near, b == 2 * far + 1 - y)
+
+        @pl.when(jnp.logical_or(jnp.logical_and(mine, jnp.logical_and(has_up, b <= e)), jnp.logical_and(low, whole_b)))
         def _():
             sent(left, up_send.at[b])
 
-        @pl.when(jnp.logical_and(mine, jnp.logical_and(has_dn, b >= e)))
+        @pl.when(jnp.logical_or(jnp.logical_and(mine, jnp.logical_and(has_dn, b >= e)), jnp.logical_and(high, whole_b)))
         def _():
             sent(left, dn_send.at[b])
 
-        @pl.when(mine)
+        @pl.when(jnp.logical_and(near_high, half_b))
+        def _():
+            sent(left, up_send.at[b], rows // 2)
+
+        @pl.when(jnp.logical_and(near_low, half_b))
+        def _():
+            sent(left, dn_send.at[b], rows // 2)
+
+        halved = jnp.logical_and(end, b == 2 * far + y)
+        skipped = jnp.logical_and(near, b == 2 * beside + y)
+
+        @pl.when(jnp.logical_and(mine, jnp.logical_not(jnp.logical_or(halved, skipped))))
         def _():
             sent(left, y_send.at[b])
+
+        @pl.when(halved)
+        def _():
+            sent(left, y_send.at[b], rows // 2)
 
         @pl.when(is_src)
         def _():
@@ -272,20 +354,21 @@
 def on_device(ne, nc, partials, gaps, arc_start, taps):
     rows, width = partials.shape
     rwidth = width * nc // ne
-    halo = taps.shape[0] - 1
-    lags = jnp.pad(taps[::-1].astype(jnp.float32), (rows - halo, rows - 1))[None, :]
-    vmem = pl.BlockSpec(memory_space=pltpu.VMEM)
+    lags = jnp.pad(taps.astype(jnp.float32), (rows, rows - taps.shape[0]))[None, :]
+    hbm = pl.BlockSpec(memory_space=pl.ANY)
     gram = pl.pallas_call(
         functools.partial(kernel, ne, nc),
-        out_shape=jax.ShapeDtypeStruct((width, rwidth), jnp.float32),
-        in_specs=[pl.BlockSpec(memory_space=pltpu.SMEM), vmem, vmem, vmem],
-        out_specs=vmem,
+        out_shape=pltpu.VMEM((width, rwidth), jnp.float32),
+        in_specs=[pl.BlockSpec(memory_space=pltpu.SMEM), hbm, hbm, hbm],
+        out_specs=pl.BlockSpec(memory_space=pltpu.VMEM),
         scratch_shapes=[
             pltpu.VMEM((ne, rows, width), jnp.bfloat16),
             pltpu.VMEM((ne, rows, rwidth), jnp.bfloat16),
             pltpu.VMEM((rows, 2 * rows), jnp.float32),
             pltpu.VMEM((rows, width), jnp.bfloat16),
             pltpu.VMEM((rows, rwidth), jnp.bfloat16),
+            pltpu.VMEM((1, rows), jnp.int32),
+            pltpu.VMEM((1, 2 * rows), jnp.float32),
             pltpu.SemaphoreType.DMA((ne, CHUNKS)),
             pltpu.SemaphoreType.DMA((ne, CHUNKS)),
             pltpu.SemaphoreType.DMA((ne,)),
@@ -293,6 +376,7 @@
             pltpu.SemaphoreType.DMA((ne,)),
             pltpu.SemaphoreType.DMA((ne,)),
             pltpu.SemaphoreType.DMA((ne, nc // 2)),
+            pltpu.SemaphoreType.DMA((3,)),
         ],
         compiler_params=pltpu.CompilerParams(
             collective_id=0, has_side_effects=True, vmem_limit_bytes=48 * 1024 * 1024

time: 126 us -> 115 us (0.913)
  the two profiles are of different devices: /device:TPU:17 before, /device:TPU:24 now
where the time goes in v2:
time: 115 us; the launch traced here: 114 us
  Pallas kernels  107 us (93%)
  other arithmetic  6.63 us (6%)
    pallas_call x1, Pallas kernels, on_device(): pl.pallas_call(functools.partial(kernel, ne, nc), out_shape=pltpu.VMEM((w...  107 us
    mul x1, other arithmetic, on_device(): return gram * (rows * ne) ** (-0.5)  5.39 us

profile of v2, /device:TPU:24, one launch (start us, length us, event | category | flops | bytes accessed | tf_op | source)
XLA Modules:
  0.0 114.4 jit_solution(11087959355620184009)
XLA Ops:
  0.7 1.2 %pad_convert_fusion = f32[512]{0:T(512)} fusion(bf16[241]{0:T(256)(128)(2,1)} %param.7), kind=kLoop, calls=%fused_computation.1 | loop fusion | flops 512 | bytes 2530 | tf_op jit(solution)/shard_map/broadcast_in_dim | solution.py:357
  1.9 107.1 %shard_map.46 = f32[2048,1024]{1,0:T(8,128)S(1)} custom-call(s32[1]{0:T(128)S(6)} %copy.5.arc_ref, s32[1,256]{1,0:T(1,128)} %bitcast.3, f32[1,512]{1,0:T(1,128)} %bitcast.2, bf16[256,2048]{1,0:T(8,128)(2,1)} %part_ref.1), custom_call_target="tpu_custom_call" | custom-call | flops 8589934592 | bytes 8388608 | tf_op jit(solution)/shard_map/pallas_call | solution.py:359
  109.0 5.4 %broadcast_multiply_fusion = f32[2048,1024]{1,0:T(8,128)} fusion(f32[2048,1024]{1,0:T(8,128)S(1)} %shard_map.46), kind=kLoop, calls=%fused_computation | loop fusion | flops 2097152 | bytes 16777216 | tf_op jit(solution)/shard_map/mul | solution.py:388

commit v3 on v2

--- a/solution.py
+++ b/solution.py
@@ -12,9 +12,9 @@
 
 
 def kernel(
-    ne, nc, arc_ref, gaps_ref, taps_ref, part_ref, out_ref,
+    ne, nc, arc_ref, gaps_ref, taps_ref, part_ref, out_ref, wl_last, wr_last,
     left, right, table, wl, wr, gaps_here, taps_here,
-    left_recv, right_recv, up_send, dn_send, y_send, sib_send, x_send, in_sem,
+    left_recv, right_recv, up_send, dn_send, y_send, sib_send, x_send, x_last, in_sem,
 ):
     rows, width = part_ref.shape
     rwidth = right.shape[2]
@@ -59,9 +59,8 @@
         greet(dn, c)
 
     greet(across, c)
-    greet(e, sib)
-    for i in range(1, nh):
-        greet(e, lax.rem(h + i, nh) * 2 + k)
+    for i in range(1, nc):
+        greet(e, lax.rem(c + i, nc))
 
     load_rows.wait()
     load_gaps.wait()
@@ -70,7 +69,16 @@
     column = jnp.sum(jnp.where(eye, gaps_here[...].astype(jnp.float32), 0.0), axis=1, keepdims=True)
     left[e] = left[e] * column.astype(jnp.bfloat16)
 
-    pl.semaphore_wait(barrier, 1 + nh + has_up.astype(jnp.int32) + has_dn.astype(jnp.int32))
+    pl.semaphore_wait(barrier, nc + has_up.astype(jnp.int32) + has_dn.astype(jnp.int32))
+
+    def slab(t):
+        both = 2 * jnp.minimum(z, nz - 1 - z)
+        alternate = jnp.where(t % 2 == 1, z - (t + 1) // 2, z + t // 2)
+        rest = jnp.where(z <= nz - 1 - z, t, nz - 1 - t)
+        middle = jnp.where(t <= both, alternate, rest)
+        return jnp.where(z <= 1, z + t, jnp.where(z >= nz - 2, z - t, middle))
+
+    b_last = 2 * slab(slabs - 1) + 1 - y
 
     def piece(buf, b, g):
         return buf.at[b, pl.ds(pl.multiple_of(g * crows, crows), crows)]
@@ -100,22 +108,20 @@
                 send_right(right_source(b, g), b, g, x_send.at[b, i - 1], lax.rem(h + i, nh) * 2 + k)
             send_right(right_source(b, g), b, g, sib_send.at[b], sib)
 
+            @pl.when(b == b_last)
+            def _():
+                for i in range(1, nh):
+                    send_right(right_source(b, g), b, g, x_last.at[i - 1], lax.rem(h + i, nh) * 2 + 1 - k)
+
     def wait_left(b, g):
         pltpu.make_async_copy(piece(left, b, g), piece(left, b, g), left_recv.at[b, g]).wait()
 
     def wait_right(b, g):
         pltpu.make_async_copy(piece(right, b, g), piece(right, b, g), right_recv.at[b, g]).wait()
 
-        @pl.when(is_relay)
+        @pl.when(jnp.logical_and(is_relay, b != b_last))
         def _():
             send_right(piece(right, b, g), b, g, sib_send.at[b], sib)
-
-    def slab(t):
-        both = 2 * jnp.minimum(z, nz - 1 - z)
-        alternate = jnp.where(t % 2 == 1, z - (t + 1) // 2, z + t // 2)
-        rest = jnp.where(z <= nz - 1 - z, t, nz - 1 - t)
-        middle = jnp.where(t <= both, alternate, rest)
-        return jnp.where(z <= 1, z + t, jnp.where(z >= nz - 2, z - t, middle))
 
     def own(g, carry):
         @pl.when(has_up)
@@ -137,8 +143,10 @@
     )
     table[...] = lags[:, :rows].T
     out_ref[...] = jnp.zeros_like(out_ref)
-
-    def whiten_and_add(b):
+    wl_last[1] = jnp.zeros((rows, width), jnp.bfloat16)
+    wr_last[1] = jnp.zeros((rows, rwidth), jnp.bfloat16)
+
+    def whiten_into(b, into_left, into_right):
         first = b * rows
         before = jnp.maximum(b - 1, 0)
         later = first + lax.broadcasted_iota(jnp.int32, (rows, 2 * rows), 0)
@@ -157,8 +165,11 @@
                 white += jnp.dot(edge, buf[before, :, cols], preferred_element_type=jnp.float32)
                 into[:, cols] = white.astype(jnp.bfloat16)
 
-        whiten(left, wl, min(512, width))
-        whiten(right, wr, min(512, rwidth))
+        whiten(left, into_left, min(512, width))
+        whiten(right, into_right, min(512, rwidth))
+
+    def whiten_and_add(b):
+        whiten_into(b, wl, wr)
 
         @pl.loop(0, width // 256)
         def _(i):
@@ -293,9 +304,15 @@
         task = jnp.where(valid_extra, extra, task)
         valid = jnp.logical_or(valid_extra, jnp.logical_or(valid_post, valid_pre))
 
-        @pl.when(valid)
+        tail = t == slabs
+
+        @pl.when(jnp.logical_and(valid, jnp.logical_not(tail)))
         def _():
             whiten_and_add(task)
+
+        @pl.when(jnp.logical_and(valid, tail))
+        def _():
+            whiten_into(task, wl_last.at[g], wr_last.at[g])
 
         return carry
 
@@ -342,25 +359,44 @@
             for i in range(1, nh):
                 sent(right, x_send.at[b, i - 1])
 
-        @pl.when(jnp.logical_or(is_src, is_relay))
+        @pl.when(jnp.logical_or(is_src, jnp.logical_and(is_relay, b != b_last)))
         def _():
             sent(right, sib_send.at[b])
 
+        @pl.when(jnp.logical_and(is_src, b == b_last))
+        def _():
+            for i in range(1, nh):
+                sent(right, x_last.at[i - 1])
+
         return carry
 
     lax.fori_loop(0, ne, drain, 0)
+
+
+def finish(tile, scale, gram_ref, wl_ref, wr_ref, out_ref):
+    cols = pl.ds(pl.multiple_of(pl.program_id(0) * tile, tile), tile)
+    total = gram_ref[cols, :]
+    for i in range(2):
+        total += lax.dot_general(
+            wl_ref[i, :, cols], wr_ref[i], (((0,), (0,)), ((), ())), preferred_element_type=jnp.float32
+        )
+    out_ref[...] = total * scale
 
 
 def on_device(ne, nc, partials, gaps, arc_start, taps):
     rows, width = partials.shape
     rwidth = width * nc // ne
     lags = jnp.pad(taps.astype(jnp.float32), (rows, rows - taps.shape[0]))[None, :]
-    hbm = pl.BlockSpec(memory_space=pl.ANY)
-    gram = pl.pallas_call(
+    hbm, vmem = pl.BlockSpec(memory_space=pl.ANY), pl.BlockSpec(memory_space=pltpu.VMEM)
+    gram, wl_last, wr_last = pl.pallas_call(
         functools.partial(kernel, ne, nc),
-        out_shape=pltpu.VMEM((width, rwidth), jnp.float32),
+        out_shape=(
+            pltpu.VMEM((width, rwidth), jnp.float32),
+            pltpu.VMEM((2, rows, width), jnp.bfloat16),
+            pltpu.VMEM((2, rows, rwidth), jnp.bfloat16),
+        ),
         in_specs=[pl.BlockSpec(memory_space=pltpu.SMEM), hbm, hbm, hbm],
-        out_specs=pl.BlockSpec(memory_space=pltpu.VMEM),
+        out_specs=(vmem, vmem, vmem),
         scratch_shapes=[
             pltpu.VMEM((ne, rows, width), jnp.bfloat16),
             pltpu.VMEM((ne, rows, rwidth), jnp.bfloat16),
@@ -376,6 +412,7 @@
             pltpu.SemaphoreType.DMA((ne,)),
             pltpu.SemaphoreType.DMA((ne,)),
             pltpu.SemaphoreType.DMA((ne, nc // 2)),
+            pltpu.SemaphoreType.DMA((nc // 2,)),
             pltpu.SemaphoreType.DMA((3,)),
         ],
         compiler_params=pltpu.CompilerParams(
@@ -385,7 +422,18 @@
             flops=2 * ne * rows * width * rwidth, bytes_accessed=4 * width * rwidth, transcendentals=0
         ),
     )(arc_start, gaps[None, :], lags, partials)
-    return gram * (rows * ne) ** (-0.5)
+    tile = min(256, width)
+    return pl.pallas_call(
+        functools.partial(finish, tile, (rows * ne) ** (-0.5)),
+        out_shape=jax.ShapeDtypeStruct((width, rwidth), jnp.float32),
+        grid=(width // tile,),
+        in_specs=[vmem, vmem, vmem],
+        out_specs=pl.BlockSpec((tile, rwidth), lambda i: (i, 0)),
+        compiler_params=pltpu.CompilerParams(vmem_limit_bytes=16 * 1024 * 1024),
+        cost_estimate=pl.CostEstimate(
+            flops=4 * rows * width * rwidth, bytes_accessed=4 * width * rwidth, transcendentals=0
+        ),
+    )(gram, wl_last, wr_last)
 
 
 def solution(mesh):

time: 115 us -> 111 us (0.965)
  other arithmetic: 6.63 us -> 1.24 us
  Pallas kernels: 107 us -> 109 us
    mul x1 -> x0, other arithmetic: 5.39 us -> none  [on_device(): return gram * (rows * ne) ** (-0.5)]
    pallas_call x1 -> x2, Pallas kernels: 107 us -> 109 us  [the longest x1 103 us: on_device(): pl.pallas_call(functools.partial(kernel, ne, nc), out_shape=(pltpu.VMEM((...]
where the time goes in v3:
time: 111 us
  Pallas kernels  109 us (98%)
  other arithmetic  1.24 us (1%)
    pallas_call x1, Pallas kernels, on_device(): pl.pallas_call(functools.partial(kernel, ne, nc), out_shape=(pltpu.VMEM((...  103 us
    pallas_call x1, Pallas kernels, on_device(): pl.pallas_call(functools.partial(finish, tile, (rows * ne) ** (-0.5)), ou...  6.36 us

profile of v3, /device:TPU:24, one launch (start us, length us, event | category | flops | bytes accessed | tf_op | source)
XLA Modules:
  0.0 110.9 jit_solution(4939883658537994974)
XLA Ops:
  0.7 1.2 %pad_convert_fusion = f32[512]{0:T(512)} fusion(bf16[241]{0:T(256)(128)(2,1)} %param.7), kind=kLoop, calls=%fused_computation | loop fusion | flops 512 | bytes 2530 | tf_op jit(solution)/shard_map/broadcast_in_dim | solution.py:389
  1.9 102.7 %shard_map.46 = (f32[2048,1024]{1,0:T(8,128)S(1)}, bf16[2,256,2048]{2,1,0:T(8,128)(2,1)S(1)}, bf16[2,256,1024]{2,1,0:T(8,128)(2,1)S(1)}) custom-call(s32[1]{0:T(128)S(6)} %copy.5.arc_ref, s32[1,256]{1,0:T(1,128)} %bitcast.3, f32[1,512]{1,0:T(1,128)} %bitcast.2, bf16[256,2048]{1,0:T(8,128)(2,1)} %part_ref.1), custom_call_target="tpu_custom_call" | custom-call | flops 8589934592 | bytes 8388608 | tf_op jit(solution)/shard_map/pallas_call | solution.py:391
  104.6 6.4 %shard_map.47 = f32[2048,1024]{1,0:T(8,128)} custom-call(f32[2048,1024]{1,0:T(8,128)S(1)} %get-tuple-element.8.gram_ref, bf16[2,256,2048]{2,1,0:T(8,128)(2,1)S(1)} %get-tuple-element.9.wl_ref, bf16[2,256,1024]{2,1,0:T(8,128)(2,1)S(1)} %get-tuple-element.10.wr_ref), custom_call_target="tpu_custom_call" | custom-call | flops 2147483648 | bytes 8388608 | tf_op jit(solution)/shard_map/pallas_call | solution.py:426

commit v4 on v3

--- a/solution.py
+++ b/solution.py
@@ -8,7 +8,7 @@
 from jax.sharding import PartitionSpec as P
 
 MESH = pl.DeviceIdType.MESH
-CHUNKS = 4
+CHUNKS = 8
 
 
 def kernel(
@@ -143,8 +143,8 @@
     )
     table[...] = lags[:, :rows].T
     out_ref[...] = jnp.zeros_like(out_ref)
-    wl_last[1] = jnp.zeros((rows, width), jnp.bfloat16)
-    wr_last[1] = jnp.zeros((rows, rwidth), jnp.bfloat16)
+    wl_last[rows:] = jnp.zeros((2 * rows, width), jnp.bfloat16)
+    wr_last[rows:] = jnp.zeros((2 * rows, rwidth), jnp.bfloat16)
 
     def whiten_into(b, into_left, into_right):
         first = b * rows
@@ -168,15 +168,21 @@
         whiten(left, into_left, min(512, width))
         whiten(right, into_right, min(512, rwidth))
 
-    def whiten_and_add(b):
-        whiten_into(b, wl, wr)
+    def add(blocks):
+        depth = pl.ds(0, blocks * rows)
 
         @pl.loop(0, width // 256)
         def _(i):
             cols = pl.ds(pl.multiple_of(i * 256, 256), 256)
             out_ref[cols, :] += lax.dot_general(
-                wl[:, cols], wr[...], (((0,), (0,)), ((), ())), preferred_element_type=jnp.float32
+                wl[depth, cols], wr[depth, :], (((0,), (0,)), ((), ())), preferred_element_type=jnp.float32
             )
+
+    def part(buf, i):
+        return buf.at[pl.ds(pl.multiple_of(i * rows, rows), rows)]
+
+    def chunk(t, g):
+        return jnp.where(jnp.logical_and(end, t == nz - 1), g % 2 * (G // 2) + g // 2, g)
 
     def step(it, carry):
         t, g = it // G, it % G
@@ -213,7 +219,7 @@
         @pl.when(t < slabs)
         def _():
             b = 2 * slab(t) + 1 - y
-            wait_left(b, g)
+            wait_left(b, chunk(t, g))
             to_near = jnp.logical_and(end, t == 0)
             to_end = jnp.logical_and(near, jnp.logical_and(t == nz - 2, g >= G // 2))
 
@@ -225,7 +231,7 @@
             def _():
                 send_left(b, g, dn_send, dn)
 
-            spread(b, g)
+            spread(b, chunk(t, g))
 
         @pl.when(jnp.logical_and(near, t == 1))
         def _():
@@ -251,7 +257,7 @@
 
         @pl.when(jnp.logical_and(it >= 1, pt < slabs))
         def _():
-            wait_right(2 * slab(pt) + 1 - y, pg)
+            wait_right(2 * slab(pt) + 1 - y, chunk(pt, pg))
 
         @pl.when(jnp.logical_and(it >= 1, jnp.logical_and(near, pt == 1)))
         def _():
@@ -275,10 +281,12 @@
         valid_pre = jnp.where(
             s_now > z, y == 0, jnp.logical_and(s_now < z, jnp.logical_or(y == 1, s_now == 0))
         )
+        quarter, on_quarter = g // (G // 4), g % (G // 4) == 0
+        at0, at1, at2, at3 = quarter == 0, quarter == 1, quarter == 2, quarter == 3
         free = jnp.where(near_low == (y == 0), 1, 2)
-        early = jnp.logical_and(t == 1, g == 3)
-        middling = jnp.logical_and(t == 2, g == free)
-        late = jnp.logical_and(t == 2, g == 3)
+        early = jnp.logical_and(t == 1, at3)
+        middling = jnp.logical_and(t == 2, quarter == free)
+        late = jnp.logical_and(t == 2, at3)
         first_low = jnp.where(y == 0, 0, 2)
         middling_low, late_low = jnp.where(y == 0, 2, 0), 1
         middling_high, late_high = ne - 2, ne - 1
@@ -297,26 +305,37 @@
         )
         valid_post = jnp.logical_and(
             jnp.logical_and(t >= 1, t <= slabs),
-            jnp.logical_or(g == 0, jnp.logical_and(g == 1, valid_b)),
-        )
-        valid_pre = jnp.logical_and(jnp.logical_and(t >= 1, t < slabs), jnp.logical_and(g == 2, valid_pre))
-        task = jnp.where(g == 0, post_a, jnp.where(g == 1, post_b, pre))
+            jnp.logical_or(at0, jnp.logical_and(at1, valid_b)),
+        )
+        valid_pre = jnp.logical_and(jnp.logical_and(t >= 1, t < slabs), jnp.logical_and(at2, valid_pre))
+        task = jnp.where(at0, post_a, jnp.where(at1, post_b, pre))
         task = jnp.where(valid_extra, extra, task)
         valid = jnp.logical_or(valid_extra, jnp.logical_or(valid_post, valid_pre))
-
-        tail = t == slabs
-
-        @pl.when(jnp.logical_and(valid, jnp.logical_not(tail)))
-        def _():
-            whiten_and_add(task)
-
-        @pl.when(jnp.logical_and(valid, tail))
-        def _():
-            whiten_into(task, wl_last.at[g], wr_last.at[g])
+        valid = jnp.logical_and(on_quarter, valid)
+
+        held = jnp.logical_or(t == slabs, jnp.logical_and(valid_pre, t == slabs - 1))
+        paired = jnp.logical_and(valid_post, valid_b)
+
+        @pl.when(jnp.logical_and(valid, jnp.logical_not(held)))
+        def _():
+            second = jnp.logical_and(paired, at1).astype(jnp.int32)
+            whiten_into(task, part(wl, second), part(wr, second))
+
+            @pl.when(jnp.logical_not(paired))
+            def _():
+                add(1)
+
+            @pl.when(jnp.logical_and(paired, at1))
+            def _():
+                add(2)
+
+        @pl.when(jnp.logical_and(valid, held))
+        def _():
+            whiten_into(task, part(wl_last, quarter), part(wr_last, quarter))
 
         return carry
 
-    lax.fori_loop(0, nz * G + 2, step, 0)
+    lax.fori_loop(0, nz * G + G // 4 + 1, step, 0)
 
     def drain(b, carry):
         def sent(buf, sem, part=rows):
@@ -373,14 +392,25 @@
     lax.fori_loop(0, ne, drain, 0)
 
 
-def finish(tile, scale, gram_ref, wl_ref, wr_ref, out_ref):
-    cols = pl.ds(pl.multiple_of(pl.program_id(0) * tile, tile), tile)
-    total = gram_ref[cols, :]
-    for i in range(2):
-        total += lax.dot_general(
-            wl_ref[i, :, cols], wr_ref[i], (((0,), (0,)), ((), ())), preferred_element_type=jnp.float32
-        )
-    out_ref[...] = total * scale
+def finish(tile, scale, gram_ref, wl_ref, wr_ref, out_ref, buf, sem):
+    tiles = gram_ref.shape[0] // tile
+
+    def write(i):
+        cols = pl.ds(pl.multiple_of(i * tile, tile), tile)
+        return pltpu.make_async_copy(buf.at[cols], out_ref.at[cols], sem.at[i])
+
+    @pl.loop(0, tiles)
+    def _(i):
+        cols = pl.ds(pl.multiple_of(i * tile, tile), tile)
+        product = lax.dot_general(
+            wl_ref[:, cols], wr_ref[...], (((0,), (0,)), ((), ())), preferred_element_type=jnp.float32
+        )
+        buf[cols, :] = (gram_ref[cols, :] + product) * scale
+        write(i).start()
+
+    @pl.loop(0, tiles)
+    def _(i):
+        write(i).wait()
 
 
 def on_device(ne, nc, partials, gaps, arc_start, taps):
@@ -392,8 +422,8 @@
         functools.partial(kernel, ne, nc),
         out_shape=(
             pltpu.VMEM((width, rwidth), jnp.float32),
-            pltpu.VMEM((2, rows, width), jnp.bfloat16),
-            pltpu.VMEM((2, rows, rwidth), jnp.bfloat16),
+            pltpu.VMEM((3 * rows, width), jnp.bfloat16),
+            pltpu.VMEM((3 * rows, rwidth), jnp.bfloat16),
         ),
         in_specs=[pl.BlockSpec(memory_space=pltpu.SMEM), hbm, hbm, hbm],
         out_specs=(vmem, vmem, vmem),
@@ -401,8 +431,8 @@
             pltpu.VMEM((ne, rows, width), jnp.bfloat16),
             pltpu.VMEM((ne, rows, rwidth), jnp.bfloat16),
             pltpu.VMEM((rows, 2 * rows), jnp.float32),
-            pltpu.VMEM((rows, width), jnp.bfloat16),
-            pltpu.VMEM((rows, rwidth), jnp.bfloat16),
+            pltpu.VMEM((2 * rows, width), jnp.bfloat16),
+            pltpu.VMEM((2 * rows, rwidth), jnp.bfloat16),
             pltpu.VMEM((1, rows), jnp.int32),
             pltpu.VMEM((1, 2 * rows), jnp.float32),
             pltpu.SemaphoreType.DMA((ne, CHUNKS)),
@@ -416,7 +446,7 @@
             pltpu.SemaphoreType.DMA((3,)),
         ],
         compiler_params=pltpu.CompilerParams(
-            collective_id=0, has_side_effects=True, vmem_limit_bytes=48 * 1024 * 1024
+            collective_id=0, has_side_effects=True, vmem_limit_bytes=44 * 1024 * 1024
         ),
         cost_estimate=pl.CostEstimate(
             flops=2 * ne * rows * width * rwidth, bytes_accessed=4 * width * rwidth, transcendentals=0
@@ -426,10 +456,13 @@
     return pl.pallas_call(
         functools.partial(finish, tile, (rows * ne) ** (-0.5)),
         out_shape=jax.ShapeDtypeStruct((width, rwidth), jnp.float32),
-        grid=(width // tile,),
         in_specs=[vmem, vmem, vmem],
-        out_specs=pl.BlockSpec((tile, rwidth), lambda i: (i, 0)),
-        compiler_params=pltpu.CompilerParams(vmem_limit_bytes=16 * 1024 * 1024),
+        out_specs=hbm,
+        scratch_shapes=[
+            pltpu.VMEM((width, rwidth), jnp.float32),
+            pltpu.SemaphoreType.DMA((width // tile,)),
+        ],
+        compiler_params=pltpu.CompilerParams(vmem_limit_bytes=24 * 1024 * 1024),
         cost_estimate=pl.CostEstimate(
             flops=4 * rows * width * rwidth, bytes_accessed=4 * width * rwidth, transcendentals=0
         ),

time: 111 us -> 106 us (0.955)
  Pallas kernels: 109 us -> 104 us
    pallas_call x1, Pallas kernels: 103 us -> 97.9 us  [on_device(): pl.pallas_call(functools.partial(kernel, ne, nc), out_shape=(pltpu.VMEM((...]
where the time goes in v4:
time: 106 us
  Pallas kernels  104 us (98%)
  other arithmetic  1.24 us (1%)
    pallas_call x1, Pallas kernels, on_device(): pl.pallas_call(functools.partial(kernel, ne, nc), out_shape=(pltpu.VMEM((...  97.9 us
    pallas_call x1, Pallas kernels, on_device(): pl.pallas_call(functools.partial(finish, tile, (rows * ne) ** (-0.5)), ou...  6.06 us

profile of v4, /device:TPU:24, one launch (start us, length us, event | category | flops | bytes accessed | tf_op | source)
XLA Modules:
  0.0 105.9 jit_solution(7530135682407128627)
XLA Ops:
  0.7 1.2 %pad_convert_fusion = f32[512]{0:T(512)} fusion(bf16[241]{0:T(256)(128)(2,1)} %param.7), kind=kLoop, calls=%fused_computation | loop fusion | flops 512 | bytes 2530 | tf_op jit(solution)/shard_map/broadcast_in_dim | solution.py:419
  1.9 97.9 %shard_map.46 = (f32[2048,1024]{1,0:T(8,128)S(1)}, bf16[768,2048]{1,0:T(8,128)(2,1)S(1)}, bf16[768,1024]{1,0:T(8,128)(2,1)S(1)}) custom-call(s32[1]{0:T(128)S(6)} %copy.5.arc_ref, s32[1,256]{1,0:T(1,128)} %bitcast.3, f32[1,512]{1,0:T(1,128)} %bitcast.2, bf16[256,2048]{1,0:T(8,128)(2,1)} %part_ref.1), custom_call_target="tpu_custom_call" | custom-call | flops 8589934592 | bytes 8388608 | tf_op jit(solution)/shard_map/pallas_call | solution.py:421
  99.8 6.1 %shard_map.47 = f32[2048,1024]{1,0:T(8,128)} custom-call(f32[2048,1024]{1,0:T(8,128)S(1)} %get-tuple-element.8.gram_ref, bf16[768,2048]{1,0:T(8,128)(2,1)S(1)} %get-tuple-element.9.wl_ref, bf16[768,1024]{1,0:T(8,128)(2,1)S(1)} %get-tuple-element.10.wr_ref), custom_call_target="tpu_custom_call" | custom-call | flops 2147483648 | bytes 8388608 | tf_op jit(solution)/shard_map/pallas_call | solution.py:456

commit v5 on v4

--- a/solution.py
+++ b/solution.py
@@ -83,6 +83,49 @@
     def piece(buf, b, g):
         return buf.at[b, pl.ds(pl.multiple_of(g * crows, crows), crows)]
 
+    halves = 2 * rwidth == width
+    groups = G // 4
+
+    def last_rows(i):
+        if not halves:
+            return pl.ds(pl.multiple_of(i * crows, crows), crows)
+        group = i // (G // 2) * groups + i % groups
+        return pl.ds(pl.multiple_of(group * 2 * crows, 2 * crows), 2 * crows)
+
+    def last_piece(b, i, ee):
+        if not halves:
+            return left.at[b, last_rows(i)]
+        second = (i % (G // 2) // groups + ee * nc % ne // nc) % 2
+        return left.at[b, last_rows(i), pl.ds(pl.multiple_of(second * rwidth, rwidth), rwidth)]
+
+    def last_spreads(i):
+        return i % (G // 2) < groups if halves else i >= 0
+
+    def send_last(b, i, sem, ee):
+        pltpu.make_async_remote_copy(
+            src_ref=last_piece(b, i, ee), dst_ref=last_piece(b, i, ee),
+            send_sem=sem.at[b], recv_sem=left_recv.at[b, i],
+            device_id=(ee, c), device_id_type=MESH,
+        ).start()
+
+    def spread_last(b, i):
+        source = left.at[b, last_rows(i), pl.ds(offset, rwidth)]
+        target = right.at[b, last_rows(i)]
+
+        def send(sem, cc):
+            pltpu.make_async_remote_copy(
+                src_ref=source, dst_ref=target, send_sem=sem, recv_sem=right_recv.at[b, i],
+                device_id=(e, cc), device_id_type=MESH,
+            ).start()
+
+        @pl.when(jnp.logical_and(is_src, last_spreads(i)))
+        def _():
+            for n in range(1, nh):
+                send(x_send.at[b, n - 1], lax.rem(h + n, nh) * 2 + k)
+                send(x_last.at[n - 1], lax.rem(h + n, nh) * 2 + 1 - k)
+            send(sib_send.at[b], sib)
+            pltpu.make_async_copy(source, target, right_recv.at[b, i]).start()
+
     def send_left(b, g, sem, ee):
         pltpu.make_async_remote_copy(
             src_ref=piece(left, b, g), dst_ref=piece(left, b, g),
@@ -182,7 +225,10 @@
         return buf.at[pl.ds(pl.multiple_of(i * rows, rows), rows)]
 
     def chunk(t, g):
-        return jnp.where(jnp.logical_and(end, t == nz - 1), g % 2 * (G // 2) + g // 2, g)
+        side = g % 2 * (G // 2) + g // 2
+        turned = (g + G // 2) % G
+        ends_last = jnp.logical_and(end, t == nz - 1)
+        return jnp.where(ends_last, side, jnp.where(jnp.logical_and(near, t == nz - 2), turned, g))
 
     def step(it, carry):
         t, g = it // G, it % G
@@ -210,26 +256,59 @@
 
             spread(b, g)
 
-        by_y = jnp.logical_or(t + 1 < nz - 1, jnp.logical_or(jnp.logical_not(end), g < G // 2))
-
-        @pl.when(jnp.logical_and(t + 1 < slabs, by_y))
-        def _():
-            send_left(2 * slab(t + 1) + y, g, y_send, across)
-
-        @pl.when(t < slabs)
+        half = G // 2
+        ends_next = jnp.logical_and(end, t + 1 == nz - 1)
+        near_next = jnp.logical_and(near, t + 1 == nz - 2)
+        near_last = jnp.logical_and(near, t == nz - 2)
+
+        @pl.when(jnp.logical_or(
+            jnp.logical_and(
+                t + 1 < slabs,
+                jnp.logical_not(jnp.logical_or(ends_next, jnp.logical_and(near_next, g < half))),
+            ),
+            jnp.logical_and(near_last, g < half),
+        ))
+        def _():
+            send_left(2 * slab(jnp.minimum(t + 1, slabs - 1)) + y, g, y_send, across)
+
+        @pl.when(jnp.logical_and(ends_next, g == half - 1))
+        def _():
+            for i in range(half):
+                send_last(2 * far + y, i, y_send, across)
+
+        ends_last = jnp.logical_and(end, t == nz - 1)
+
+        @pl.when(ends_last)
+        def _():
+            i = chunk(t, g)
+            piece_here = last_piece(b_last, i, e)
+            pltpu.make_async_copy(piece_here, piece_here, left_recv.at[b_last, i]).wait()
+            spread_last(b_last, i)
+
+        @pl.when(jnp.logical_and(t < slabs, jnp.logical_not(ends_last)))
         def _():
             b = 2 * slab(t) + 1 - y
             wait_left(b, chunk(t, g))
             to_near = jnp.logical_and(end, t == 0)
-            to_end = jnp.logical_and(near, jnp.logical_and(t == nz - 2, g >= G // 2))
-
-            @pl.when(jnp.logical_or(jnp.logical_and(low, to_near), jnp.logical_and(near_high, to_end)))
+            to_end = jnp.logical_and(near_last, g == half - 1)
+
+            @pl.when(jnp.logical_and(low, to_near))
             def _():
                 send_left(b, g, up_send, up)
 
-            @pl.when(jnp.logical_or(jnp.logical_and(high, to_near), jnp.logical_and(near_low, to_end)))
+            @pl.when(jnp.logical_and(high, to_near))
             def _():
                 send_left(b, g, dn_send, dn)
+
+            @pl.when(jnp.logical_and(near_high, to_end))
+            def _():
+                for i in range(half, G):
+                    send_last(b, i, up_send, up)
+
+            @pl.when(jnp.logical_and(near_low, to_end))
+            def _():
+                for i in range(half, G):
+                    send_last(b, i, dn_send, dn)
 
             spread(b, chunk(t, g))
 
@@ -255,9 +334,17 @@
         def _():
             wait_right(e + 2 * (pt + 1), pg)
 
-        @pl.when(jnp.logical_and(it >= 1, pt < slabs))
+        ends_past = jnp.logical_and(end, pt == nz - 1)
+
+        @pl.when(jnp.logical_and(it >= 1, jnp.logical_and(pt < slabs, jnp.logical_not(ends_past))))
         def _():
             wait_right(2 * slab(pt) + 1 - y, chunk(pt, pg))
+
+        @pl.when(jnp.logical_and(ends_past, last_spreads(chunk(pt, pg))))
+        def _():
+            i = chunk(pt, pg)
+            rows_here = right.at[b_last, last_rows(i)]
+            pltpu.make_async_copy(rows_here, rows_here, right_recv.at[b_last, i]).wait()
 
         @pl.when(jnp.logical_and(it >= 1, jnp.logical_and(near, pt == 1)))
         def _():

time: 106 us -> 106 us (level)
  no operation moved by 1% of the time
where the time goes in v5:
time: 106 us; the launch traced here: 105 us
  Pallas kernels  103 us (97%)
  other arithmetic  1.24 us (1%)
    pallas_call x1, Pallas kernels, on_device(): pl.pallas_call(functools.partial(kernel, ne, nc), out_shape=(pltpu.VMEM((...  97.3 us
    pallas_call x1, Pallas kernels, on_device(): pl.pallas_call(functools.partial(finish, tile, (rows * ne) ** (-0.5)), ou...  6.06 us

profile of v5, /device:TPU:24, one launch (start us, length us, event | category | flops | bytes accessed | tf_op | source)
XLA Modules:
  0.0 105.3 jit_solution(2691420003168089988)
XLA Ops:
  0.7 1.2 %pad_convert_fusion = f32[512]{0:T(512)} fusion(bf16[241]{0:T(256)(128)(2,1)} %param.7), kind=kLoop, calls=%fused_computation | loop fusion | flops 512 | bytes 2530 | tf_op jit(solution)/shard_map/broadcast_in_dim | solution.py:506
  1.9 97.3 %shard_map.46 = (f32[2048,1024]{1,0:T(8,128)S(1)}, bf16[768,2048]{1,0:T(8,128)(2,1)S(1)}, bf16[768,1024]{1,0:T(8,128)(2,1)S(1)}) custom-call(s32[1]{0:T(128)S(6)} %copy.5.arc_ref, s32[1,256]{1,0:T(1,128)} %bitcast.3, f32[1,512]{1,0:T(1,128)} %bitcast.2, bf16[256,2048]{1,0:T(8,128)(2,1)} %part_ref.1), custom_call_target="tpu_custom_call" | custom-call | flops 8589934592 | bytes 8388608 | tf_op jit(solution)/shard_map/pallas_call | solution.py:508
  99.2 6.1 %shard_map.47 = f32[2048,1024]{1,0:T(8,128)} custom-call(f32[2048,1024]{1,0:T(8,128)S(1)} %get-tuple-element.8.gram_ref, bf16[768,2048]{1,0:T(8,128)(2,1)S(1)} %get-tuple-element.9.wl_ref, bf16[768,1024]{1,0:T(8,128)(2,1)S(1)} %get-tuple-element.10.wr_ref), custom_call_target="tpu_custom_call" | custom-call | flops 2147483648 | bytes 8388608 | tf_op jit(solution)/shard_map/pallas_call | solution.py:543

commit v6 on v5

--- a/solution.py
+++ b/solution.py
@@ -13,12 +13,13 @@
 
 def kernel(
     ne, nc, arc_ref, gaps_ref, taps_ref, part_ref, out_ref, wl_last, wr_last,
-    left, right, table, wl, wr, gaps_here, taps_here,
-    left_recv, right_recv, up_send, dn_send, y_send, sib_send, x_send, x_last, in_sem,
+    left_all, right_all, table, wl, wr, gaps_here, taps_here,
+    left_recv, right_recv, up_send, dn_send, y_send, sib_send, x_send, in_sem,
 ):
     rows, width = part_ref.shape
-    rwidth = right.shape[2]
+    rwidth = right_all.shape[2]
     nz, nh = ne // 2, nc // 2
+    left, right = left_all.at[pl.ds(1, ne)], right_all.at[pl.ds(1, ne)]
     G = CHUNKS
     crows = rows // G
     e, c = lax.axis_index("epoch"), lax.axis_index("col")
@@ -122,7 +123,6 @@
         def _():
             for n in range(1, nh):
                 send(x_send.at[b, n - 1], lax.rem(h + n, nh) * 2 + k)
-                send(x_last.at[n - 1], lax.rem(h + n, nh) * 2 + 1 - k)
             send(sib_send.at[b], sib)
             pltpu.make_async_copy(source, target, right_recv.at[b, i]).start()
 
@@ -151,18 +151,13 @@
                 send_right(right_source(b, g), b, g, x_send.at[b, i - 1], lax.rem(h + i, nh) * 2 + k)
             send_right(right_source(b, g), b, g, sib_send.at[b], sib)
 
-            @pl.when(b == b_last)
-            def _():
-                for i in range(1, nh):
-                    send_right(right_source(b, g), b, g, x_last.at[i - 1], lax.rem(h + i, nh) * 2 + 1 - k)
-
     def wait_left(b, g):
         pltpu.make_async_copy(piece(left, b, g), piece(left, b, g), left_recv.at[b, g]).wait()
 
     def wait_right(b, g):
         pltpu.make_async_copy(piece(right, b, g), piece(right, b, g), right_recv.at[b, g]).wait()
 
-        @pl.when(jnp.logical_and(is_relay, b != b_last))
+        @pl.when(is_relay)
         def _():
             send_right(piece(right, b, g), b, g, sib_send.at[b], sib)
 
@@ -185,31 +180,31 @@
         jnp.broadcast_to(taps_here[...], (2 * rows, 2 * rows)), 0, 1, stride=1, stride_axis=0
     )
     table[...] = lags[:, :rows].T
+    left_all[0] = jnp.zeros((rows, width), jnp.bfloat16)
+    right_all[0] = jnp.zeros((rows, rwidth), jnp.bfloat16)
     out_ref[...] = jnp.zeros_like(out_ref)
     wl_last[rows:] = jnp.zeros((2 * rows, width), jnp.bfloat16)
     wr_last[rows:] = jnp.zeros((2 * rows, rwidth), jnp.bfloat16)
 
     def whiten_into(b, into_left, into_right):
         first = b * rows
-        before = jnp.maximum(b - 1, 0)
         later = first + lax.broadcasted_iota(jnp.int32, (rows, 2 * rows), 0)
         source = first - rows + lax.broadcasted_iota(jnp.int32, (rows, 2 * rows), 1)
         boundary = arc_ref[0]
         same = (later >= boundary) == (source >= boundary)
         keep = jnp.logical_and(same, source >= 0)
         taps = jnp.where(keep, table[...], 0.0).astype(jnp.bfloat16)
-        edge, inner = taps[:, :rows], taps[:, rows:]
 
         def whiten(buf, into, step):
             @pl.loop(0, into.shape[1] // step)
             def _(i):
                 cols = pl.ds(pl.multiple_of(i * step, step), step)
-                white = jnp.dot(inner, buf[b, :, cols], preferred_element_type=jnp.float32)
-                white += jnp.dot(edge, buf[before, :, cols], preferred_element_type=jnp.float32)
+                both = buf[pl.ds(b, 2), :, cols].reshape(2 * rows, step)
+                white = jnp.dot(taps, both, preferred_element_type=jnp.float32)
                 into[:, cols] = white.astype(jnp.bfloat16)
 
-        whiten(left, into_left, min(512, width))
-        whiten(right, into_right, min(512, rwidth))
+        whiten(left_all, into_left, min(512, width))
+        whiten(right_all, into_right, min(512, rwidth))
 
     def add(blocks):
         depth = pl.ds(0, blocks * rows)
@@ -345,6 +340,14 @@
             i = chunk(pt, pg)
             rows_here = right.at[b_last, last_rows(i)]
             pltpu.make_async_copy(rows_here, rows_here, right_recv.at[b_last, i]).wait()
+
+            @pl.when(is_relay)
+            def _():
+                pltpu.make_async_remote_copy(
+                    src_ref=rows_here, dst_ref=rows_here,
+                    send_sem=sib_send.at[b_last], recv_sem=right_recv.at[b_last, i],
+                    device_id=(e, sib), device_id_type=MESH,
+                ).start()
 
         @pl.when(jnp.logical_and(it >= 1, jnp.logical_and(near, pt == 1)))
         def _():
@@ -465,14 +468,9 @@
             for i in range(1, nh):
                 sent(right, x_send.at[b, i - 1])
 
-        @pl.when(jnp.logical_or(is_src, jnp.logical_and(is_relay, b != b_last)))
+        @pl.when(jnp.logical_or(is_src, is_relay))
         def _():
             sent(right, sib_send.at[b])
-
-        @pl.when(jnp.logical_and(is_src, b == b_last))
-        def _():
-            for i in range(1, nh):
-                sent(right, x_last.at[i - 1])
 
         return carry
 
@@ -515,8 +513,8 @@
         in_specs=[pl.BlockSpec(memory_space=pltpu.SMEM), hbm, hbm, hbm],
         out_specs=(vmem, vmem, vmem),
         scratch_shapes=[
-            pltpu.VMEM((ne, rows, width), jnp.bfloat16),
-            pltpu.VMEM((ne, rows, rwidth), jnp.bfloat16),
+            pltpu.VMEM((ne + 1, rows, width), jnp.bfloat16),
+            pltpu.VMEM((ne + 1, rows, rwidth), jnp.bfloat16),
             pltpu.VMEM((rows, 2 * rows), jnp.float32),
             pltpu.VMEM((2 * rows, width), jnp.bfloat16),
             pltpu.VMEM((2 * rows, rwidth), jnp.bfloat16),
@@ -529,7 +527,6 @@
             pltpu.SemaphoreType.DMA((ne,)),
             pltpu.SemaphoreType.DMA((ne,)),
             pltpu.SemaphoreType.DMA((ne, nc // 2)),
-            pltpu.SemaphoreType.DMA((nc // 2,)),
             pltpu.SemaphoreType.DMA((3,)),
         ],
         compiler_params=pltpu.CompilerParams(

time: 106 us -> 105 us (level)
  no operation moved by 1% of the time
where the time goes in v6:
time: 105 us
  Pallas kernels  103 us (98%)
  other arithmetic  1.24 us (1%)
    pallas_call x1, Pallas kernels, on_device(): pl.pallas_call(functools.partial(kernel, ne, nc), out_shape=(pltpu.VMEM((...  96.6 us
    pallas_call x1, Pallas kernels, on_device(): pl.pallas_call(functools.partial(finish, tile, (rows * ne) ** (-0.5)), ou...  6.06 us

profile of v6, /device:TPU:24, one launch (start us, length us, event | category | flops | bytes accessed | tf_op | source)
XLA Modules:
  0.0 104.6 jit_solution(11685400412537181366)
XLA Ops:
  0.7 1.2 %pad_convert_fusion = f32[512]{0:T(512)} fusion(bf16[241]{0:T(256)(128)(2,1)} %param.7), kind=kLoop, calls=%fused_computation | loop fusion | flops 512 | bytes 2530 | tf_op jit(solution)/shard_map/broadcast_in_dim | solution.py:504
  1.9 96.6 %shard_map.46 = (f32[2048,1024]{1,0:T(8,128)S(1)}, bf16[768,2048]{1,0:T(8,128)(2,1)S(1)}, bf16[768,1024]{1,0:T(8,128)(2,1)S(1)}) custom-call(s32[1]{0:T(128)S(6)} %copy.5.arc_ref, s32[1,256]{1,0:T(1,128)} %bitcast.3, f32[1,512]{1,0:T(1,128)} %bitcast.2, bf16[256,2048]{1,0:T(8,128)(2,1)} %part_ref.1), custom_call_target="tpu_custom_call" | custom-call | flops 8589934592 | bytes 8388608 | tf_op jit(solution)/shard_map/pallas_call | solution.py:506
  98.5 6.1 %shard_map.47 = f32[2048,1024]{1,0:T(8,128)} custom-call(f32[2048,1024]{1,0:T(8,128)S(1)} %get-tuple-element.8.gram_ref, bf16[768,2048]{1,0:T(8,128)(2,1)S(1)} %get-tuple-element.9.wl_ref, bf16[768,1024]{1,0:T(8,128)(2,1)S(1)} %get-tuple-element.10.wr_ref), custom_call_target="tpu_custom_call" | custom-call | flops 2147483648 | bytes 8388608 | tf_op jit(solution)/shard_map/pallas_call | solution.py:540

commit v7 on v6

--- a/solution.py
+++ b/solution.py
@@ -146,10 +146,10 @@
     def spread(b, g):
         @pl.when(is_src)
         def _():
-            pltpu.make_async_copy(right_source(b, g), piece(right, b, g), right_recv.at[b, g]).start()
             for i in range(1, nh):
                 send_right(right_source(b, g), b, g, x_send.at[b, i - 1], lax.rem(h + i, nh) * 2 + k)
             send_right(right_source(b, g), b, g, sib_send.at[b], sib)
+            pltpu.make_async_copy(right_source(b, g), piece(right, b, g), right_recv.at[b, g]).start()
 
     def wait_left(b, g):
         pltpu.make_async_copy(piece(left, b, g), piece(left, b, g), left_recv.at[b, g]).wait()
@@ -229,6 +229,46 @@
         t, g = it // G, it % G
         moving = t < nz
 
+        @pl.when(t == 0)
+        def _():
+            wait_right(e, g)
+
+        last = jnp.maximum(it - 1, 0)
+        pt, pg = last // G, last % G
+        passed = jnp.logical_and(it >= 1, pt < nz)
+
+        @pl.when(jnp.logical_and(passed, z - pt - 1 >= 0))
+        def _():
+            wait_right(e - 2 * (pt + 1), pg)
+
+        @pl.when(jnp.logical_and(passed, z + pt + 1 < nz))
+        def _():
+            wait_right(e + 2 * (pt + 1), pg)
+
+        ends_past = jnp.logical_and(end, pt == nz - 1)
+
+        @pl.when(jnp.logical_and(it >= 1, jnp.logical_and(pt < slabs, jnp.logical_not(ends_past))))
+        def _():
+            wait_right(2 * slab(pt) + 1 - y, chunk(pt, pg))
+
+        @pl.when(jnp.logical_and(ends_past, last_spreads(chunk(pt, pg))))
+        def _():
+            i = chunk(pt, pg)
+            rows_here = right.at[b_last, last_rows(i)]
+            pltpu.make_async_copy(rows_here, rows_here, right_recv.at[b_last, i]).wait()
+
+            @pl.when(is_relay)
+            def _():
+                pltpu.make_async_remote_copy(
+                    src_ref=rows_here, dst_ref=rows_here,
+                    send_sem=sib_send.at[b_last], recv_sem=right_recv.at[b_last, i],
+                    device_id=(e, sib), device_id_type=MESH,
+                ).start()
+
+        @pl.when(jnp.logical_and(it >= 1, jnp.logical_and(near, pt == 1)))
+        def _():
+            wait_right(2 * beside + 1 - y, pg)
+
         @pl.when(jnp.logical_and(moving, z - t - 1 >= 0))
         def _():
             b = e - 2 * (t + 1)
@@ -312,46 +352,6 @@
             b = 2 * beside + 1 - y
             wait_left(b, g)
             spread(b, g)
-
-        @pl.when(t == 0)
-        def _():
-            wait_right(e, g)
-
-        last = jnp.maximum(it - 1, 0)
-        pt, pg = last // G, last % G
-        passed = jnp.logical_and(it >= 1, pt < nz)
-
-        @pl.when(jnp.logical_and(passed, z - pt - 1 >= 0))
-        def _():
-            wait_right(e - 2 * (pt + 1), pg)
-
-        @pl.when(jnp.logical_and(passed, z + pt + 1 < nz))
-        def _():
-            wait_right(e + 2 * (pt + 1), pg)
-
-        ends_past = jnp.logical_and(end, pt == nz - 1)
-
-        @pl.when(jnp.logical_and(it >= 1, jnp.logical_and(pt < slabs, jnp.logical_not(ends_past))))
-        def _():
-            wait_right(2 * slab(pt) + 1 - y, chunk(pt, pg))
-
-        @pl.when(jnp.logical_and(ends_past, last_spreads(chunk(pt, pg))))
-        def _():
-            i = chunk(pt, pg)
-            rows_here = right.at[b_last, last_rows(i)]
-            pltpu.make_async_copy(rows_here, rows_here, right_recv.at[b_last, i]).wait()
-
-            @pl.when(is_relay)
-            def _():
-                pltpu.make_async_remote_copy(
-                    src_ref=rows_here, dst_ref=rows_here,
-                    send_sem=sib_send.at[b_last], recv_sem=right_recv.at[b_last, i],
-                    device_id=(e, sib), device_id_type=MESH,
-                ).start()
-
-        @pl.when(jnp.logical_and(it >= 1, jnp.logical_and(near, pt == 1)))
-        def _():
-            wait_right(2 * beside + 1 - y, pg)
 
         s = slab(jnp.clip(t - 1, 0, slabs - 1))
         s_now = slab(jnp.minimum(t, slabs - 1))

time: 105 us -> 105 us (level)
  no operation moved by 1% of the time
where the time goes in v7:
time: 105 us
  Pallas kernels  103 us (98%)
  other arithmetic  1.24 us (1%)
    pallas_call x1, Pallas kernels, on_device(): pl.pallas_call(functools.partial(kernel, ne, nc), out_shape=(pltpu.VMEM((...  96.6 us
    pallas_call x1, Pallas kernels, on_device(): pl.pallas_call(functools.partial(finish, tile, (rows * ne) ** (-0.5)), ou...  6.06 us

profile of v7, /device:TPU:24, one launch (start us, length us, event | category | flops | bytes accessed | tf_op | source)
XLA Modules:
  0.0 104.6 jit_solution(9772817170866065282)
XLA Ops:
  0.7 1.2 %pad_convert_fusion = f32[512]{0:T(512)} fusion(bf16[241]{0:T(256)(128)(2,1)} %param.7), kind=kLoop, calls=%fused_computation | loop fusion | flops 512 | bytes 2530 | tf_op jit(solution)/shard_map/broadcast_in_dim | solution.py:504
  1.9 96.6 %shard_map.46 = (f32[2048,1024]{1,0:T(8,128)S(1)}, bf16[768,2048]{1,0:T(8,128)(2,1)S(1)}, bf16[768,1024]{1,0:T(8,128)(2,1)S(1)}) custom-call(s32[1]{0:T(128)S(6)} %copy.5.arc_ref, s32[1,256]{1,0:T(1,128)} %bitcast.3, f32[1,512]{1,0:T(1,128)} %bitcast.2, bf16[256,2048]{1,0:T(8,128)(2,1)} %part_ref.1), custom_call_target="tpu_custom_call" | custom-call | flops 8589934592 | bytes 8388608 | tf_op jit(solution)/shard_map/pallas_call | solution.py:506
  98.5 6.1 %shard_map.47 = f32[2048,1024]{1,0:T(8,128)} custom-call(f32[2048,1024]{1,0:T(8,128)S(1)} %get-tuple-element.8.gram_ref, bf16[768,2048]{1,0:T(8,128)(2,1)S(1)} %get-tuple-element.9.wl_ref, bf16[768,1024]{1,0:T(8,128)(2,1)S(1)} %get-tuple-element.10.wr_ref), custom_call_target="tpu_custom_call" | custom-call | flops 2147483648 | bytes 8388608 | tf_op jit(solution)/shard_map/pallas_call | solution.py:540
